TPU v7x, 32 devices: a whole 2x2x4 slice. The times are simulated.
32 devices in a mesh: owner: 8 (over z, y), blk: 4 (over x, core).
Axes of the slice: x: 2, y: 2, z: 4, core: 2. Of those that a mesh axis runs over, the one named last changes fastest.
Arguments:
- entity_table: bfloat16 [32768, 256], P('owner'), may hold values from -1.5 to 1.5
- relations: bfloat16 [8, 256, 256], replicated, may hold values from -0.375 to 0.375
- head_ids: int32 [32768], P(('owner', 'blk')), may hold values from 0 to 32767, as said below
- rel_ids: int32 [32768], P(('owner', 'blk')), may hold values from 0 to 7
- tail_ids: int32 [32768], P(('owner', 'blk')), may hold values from 0 to 32767, as said below
- neg_ids: int32 [16384], P(('owner', 'blk')), may hold values from 0 to 32767, as said below
Outputs:
- entity_grad: float32 [32768, 256], P(('owner', 'blk'))
- relation_grad: float32 [8, 256, 256], P('blk')
Inputs may be any that keep to these rules, and one draw needn't show every extreme that they name: An entity is held by the owner index whose shard of entity_table contains its row. A device's ids are its own shards of head_ids, tail_ids and neg_ids together. Of these ids every owner holds at most 800 (800), and some owner holds exactly 800; that owner is the same for all devices of one blk index. `tail_ids`: as for head_ids: the same bound of 800 ids of one device for one owner, over the device's heads, tails and negatives together. `neg_ids`: as for head_ids: the same bound of 800 ids of one device for one owner, over the device's heads, tails and negatives together.
All inputs are finite; a program needn't handle non-finite values.
Results may differ from a plain program's by a relative error of at most 0.0027.
Values may be sent and summed in bfloat16 or wider, within the bound.
A program may use at most 64 MiB of HBM per device.

v0:
```python
import jax
import jax.numpy as jnp
from jax import lax
from jax.sharding import PartitionSpec as P


def earlier(count):
    place = jnp.arange(count, dtype=jnp.int32)
    return (place[:, None] > place[None, :]).astype(jnp.bfloat16)


def ranks(onehot):
    ids, owner_count = onehot.shape
    run = 128
    runs = onehot.reshape(ids // run, run, owner_count)
    within = jnp.einsum("ij,bjo->bio", earlier(run), runs, preferred_element_type=jnp.float32)
    totals = jnp.sum(runs.astype(jnp.float32), axis=1).astype(jnp.bfloat16)
    carried = jnp.dot(earlier(ids // run), totals, preferred_element_type=jnp.float32)
    before = within + carried[:, None, :]
    return jnp.sum(before * runs.astype(jnp.float32), axis=2).reshape(ids).astype(jnp.int32)


def group_sums(rows, grads, entity_rows):
    members = lax.axis_size("blk")
    pairs = members // 2
    size = entity_rows // members
    me = lax.axis_index("blk")
    pair, core = me // 2, me % 2
    swap = [(i, i ^ 1) for i in range(members)]

    def block(index):
        wanted = index * size + jnp.arange(size, dtype=jnp.int32)
        landing = (wanted[:, None] == rows[None, :]).astype(jnp.bfloat16)
        return jnp.dot(landing, grads, preferred_element_type=jnp.float32)

    arrived = []
    for step in range(1, pairs + 1):
        target = (pair + step) % pairs
        other = lax.ppermute(block(2 * target + 1 - core), "blk", swap)
        total = block(2 * target + core) + other
        if step < pairs:
            route = [(i, (i + 2 * step) % members) for i in range(members)]
            arrived.append(lax.ppermute(total.astype(jnp.bfloat16), "blk", route))
    for part in arrived:
        total = total + part.astype(jnp.float32)
    return total


def shards(entity_table, relations, head_ids, rel_ids, tail_ids, neg_ids):
    owner_count = lax.axis_size("owner")
    cycle_count = lax.axis_size("blk")
    entity_rows, feature_count = entity_table.shape
    triple_count = head_ids.shape[0]
    negative_count = neg_ids.shape[0]
    relation_count = relations.shape[0]
    wanted = jnp.concatenate([head_ids, tail_ids, neg_ids])
    wanted_count = wanted.shape[0]
    capacity = 5 * wanted_count // (2 * owner_count)
    owners = wanted // entity_rows
    local_rows = wanted % entity_rows
    onehot = (owners[:, None] == jnp.arange(owner_count, dtype=jnp.int32)[None, :]).astype(
        jnp.bfloat16
    )
    slot_index = ranks(onehot)
    target = owners * capacity + slot_index
    slots = jnp.arange(owner_count * capacity, dtype=jnp.int32)
    packing = (slots[:, None] == target[None, :]).astype(jnp.bfloat16)
    digits = jnp.stack([local_rows // 64, local_rows % 64], axis=1).astype(jnp.bfloat16)
    packed = jnp.dot(packing, digits, preferred_element_type=jnp.float32).astype(jnp.int32)
    requests = (packed[:, 0] * 64 + packed[:, 1]).reshape(owner_count, capacity)
    asked_rows = lax.all_to_all(requests, "owner", split_axis=0, concat_axis=0, tiled=True)
    found_rows = entity_table.at[asked_rows].get(mode="promise_in_bounds")
    fetched, asked_rows = (
        lax.all_to_all(found_rows, "owner", split_axis=0, concat_axis=0, tiled=True),
        asked_rows,
    )
    fetched_rows = fetched.reshape(owner_count * capacity, feature_count)
    fetched_rows = fetched_rows.at[target].get(mode="promise_in_bounds")
    head_rows = fetched_rows[:triple_count]
    tail_rows = fetched_rows[triple_count : 2 * triple_count]
    negative_rows = fetched_rows[2 * triple_count :]
    routes = [[(i, i ^ step) for i in range(cycle_count)] for step in range(cycle_count)]
    visitors = [negative_rows]
    for step in range(1, cycle_count):
        visitors.append(lax.ppermute(negative_rows, "blk", routes[step]))
    relation_hot = (
        rel_ids[:, None] == jnp.arange(relation_count, dtype=jnp.int32)[None, :]
    ).astype(jnp.bfloat16)
    spread_heads = (head_rows[:, None, :] * relation_hot[:, :, None]).reshape(
        triple_count, relation_count * feature_count
    )
    flat_relations = relations.reshape(relation_count * feature_count, feature_count)
    queries = jnp.dot(spread_heads, flat_relations, preferred_element_type=jnp.float32).astype(
        jnp.bfloat16
    )
    positive = jnp.einsum("id,id->i", queries, tail_rows, preferred_element_type=jnp.float32)
    slopes = -jax.nn.sigmoid(-positive)
    scale_neg = (cycle_count * negative_count) ** (-0.5)
    partner = slopes[:, None] * tail_rows.astype(jnp.float32)
    contract_rows = (((0,), (0,)), ((), ()))
    contract_cols = (((1,), (1,)), ((), ()))
    returning = []
    for step, visitor in enumerate(visitors):
        scores = lax.dot_general(
            queries, visitor, contract_cols, preferred_element_type=jnp.float32
        )
        weights = (scale_neg * jax.nn.sigmoid(scores)).astype(jnp.bfloat16)
        partner = partner + jnp.dot(weights, visitor, preferred_element_type=jnp.float32)
        sums = lax.dot_general(weights, queries, contract_rows, preferred_element_type=jnp.float32)
        if step == 0:
            collected = sums
        else:
            returning.append(lax.ppermute(sums.astype(jnp.bfloat16), "blk", routes[step]))
    partner_low = partner.astype(jnp.bfloat16)
    spread_partner = partner_low[:, None, :] * relation_hot[:, :, None]
    head_grad = jnp.einsum(
        "ire,rde->id", spread_partner, relations, preferred_element_type=jnp.float32
    )
    tail_grad = slopes[:, None] * queries.astype(jnp.float32)
    rel_term = lax.dot_general(
        spread_heads, partner_low, contract_rows, preferred_element_type=jnp.float32
    )
    rel_term = rel_term.reshape(relation_count, feature_count, feature_count)
    triple_grads = jnp.concatenate([head_grad, tail_grad], axis=0).astype(jnp.bfloat16)
    outgoing = jnp.dot(
        packing[:, : 2 * triple_count], triple_grads, preferred_element_type=jnp.float32
    ).astype(jnp.bfloat16)
    for part in returning:
        collected = collected + part.astype(jnp.float32)
    outgoing = outgoing + jnp.dot(
        packing[:, 2 * triple_count :],
        collected.astype(jnp.bfloat16),
        preferred_element_type=jnp.float32,
    ).astype(jnp.bfloat16)
    outgoing = outgoing.reshape(owner_count, capacity, feature_count)
    returned = lax.all_to_all(outgoing, "owner", split_axis=0, concat_axis=0, tiled=True)
    ent_grad = group_sums(asked_rows.reshape(-1), returned.reshape(-1, feature_count), entity_rows)
    summed_group = lax.psum_scatter(rel_term, "blk", scatter_dimension=0, tiled=True)
    gathered = lax.all_gather(summed_group.astype(jnp.bfloat16), "owner")
    rel_grad = jnp.sum(gathered.astype(jnp.float32), axis=0)
    return (ent_grad, rel_grad)


def solution(mesh):
    placed = (
        P("owner", None),
        P(),
        P(("owner", "blk")),
        P(("owner", "blk")),
        P(("owner", "blk")),
        P(("owner", "blk")),
    )
    return jax.shard_map(
        shards,
        mesh=mesh,
        in_specs=placed,
        out_specs=(P(("owner", "blk"), None), P("blk", None, None)),
        check_vma=False,
    )
```

profile of v0, /device:TPU:0, one launch (start us, length us, event | category | flops | bytes accessed | tf_op | source)
XLA Modules:
  0.0 339.2 jit_solution(1927096748824482301)
XLA Ops:
  7.2 0.8 constant_dynamic-update-slice_fusion.2
  8.0 0.7 constant_dynamic-update-slice_fusion.1
  8.7 0.7 constant_dynamic-update-slice_fusion
  9.4 0.8 fusion.102
  10.8 11.4 %convolution_convert_fusion = s32[6400,2]{0,1:T(2,128)S(1)} fusion(s32[2560]{0:T(1024)S(1)} %fusion.86, bf16[2560,1]{0,1:T(2,128)(2,1)S(1)} %fusion.93, bf16[2560,1]{0,1:T(2,128)(2,1)S(1)} %get-tuple-element.4), kind=kOutput, calls=%fused_computation.26 | convolution fusion | flops 81953280 | bytes 71680 | tf_op jit(solution)/shard_map/dot_general | solution.py:69
  22.5 13.7 %all_to_all.19 = s32[8,1,800]{2,1,0:T(1,128)S(1)} all-to-all(s32[8,1,800]{2,1,0:T(1,128)S(1)} %add.284), channel_id=1, replica_groups=mesh['owner'=8,'blk'=4] {'owner'}, dimensions={0} | all-to-all | bytes 51200 | tf_op jit(solution)/shard_map/all_to_all | solution.py:71
  36.4 18.6 %gather_fusion = bf16[6400,256]{1,0:T(8,128)(2,1)} fusion(bf16[4096,256]{1,0:T(8,128)(2,1)S(1)} %copy-done, s32[7168]{0:T(1024)S(1)} %pad_clamp_fusion), kind=kCustom, calls=%fused_computation | custom fusion | bytes 6579200 | tf_op jit(solution)/shard_map/gather | solution.py:72
  55.0 4.8 %all-to-all-start.1 = ((bf16[8,800,256]{2,1,0:T(8,128)(2,1)}), bf16[8,800,256]{2,1,0:T(8,128)(2,1)}, u32[]{:S(2)}, u32[]{:S(2)}) async-start(bf16[8,800,256]{2,1,0:T(8,128)(2,1)} %bitcast.93), calls=%async_computation.1 | async-start | bytes 6553600 | tf_op jit(solution)/shard_map/all_to_all | solution.py:74
  59.8 14.4 %iota_compare_fusion = pred[6400,2560]{1,0:T(32,128)(4,1)} fusion(s32[2560]{0:T(1024)S(1)} %fusion.86), kind=kLoop, calls=%fused_computation.2 | loop fusion | flops 16384000 | bytes 16394240 | tf_op jit(solution)/shard_map/eq | solution.py:67
  74.2 57.9 %all-to-all-done.1 = bf16[8,800,256]{2,1,0:T(8,128)(2,1)} async-done(((bf16[8,800,256]{2,1,0:T(8,128)(2,1)}), bf16[8,800,256]{2,1,0:T(8,128)(2,1)}, u32[]{:S(2)}, u32[]{:S(2)}) %all-to-all-start.1) | async-done | bytes 3276832 | tf_op jit(solution)/shard_map/all_to_all | solution.py:74
  132.1 8.1 %gather_fusion.1 = bf16[2560,256]{1,0:T(8,128)(2,1)S(1)} fusion(bf16[6400,256]{1,0:T(8,128)(2,1)} %bitcast.8, s32[3072]{0:T(1024)S(1)} %pad_clamp_fusion.1), kind=kCustom, calls=%fused_computation.1 | custom fusion | bytes 2631680 | tf_op jit(solution)/shard_map/gather | solution.py:78
  140.2 0.7 slice.37
  140.9 1.6 collective-permute-start.2
  142.5 0.5 collective-permute-start.1
  143.1 0.8 slice.35
  143.9 2.1 copy.15
  146.0 2.8 fusion.70
  148.7 0.8 multiply_convert_fusion.3
  149.5 0.4 convolution_add_fusion.1
  150.0 1.0 fusion.71
  151.0 1.7 multiply_convert_fusion
  152.7 1.2 convolution_convert_fusion.1
  153.9 0.8 collective-permute-start.5
  154.7 0.8 collective-permute-done.1
  155.5 1.7 multiply_convert_fusion.1
  157.2 1.2 convolution_convert_fusion.2
  158.4 1.5 collective-permute-start.4
  159.9 1.7 multiply_convert_fusion.2
  161.6 1.2 convolution_convert_fusion.3
  162.8 1.4 fusion.106
  164.2 1.4 fusion.105
  165.6 1.4 fusion.60
  167.2 2.6 fusion.64
  169.8 11.3 %fusion.23 = bf16[6400,256]{1,0:T(8,128)(2,1)} fusion(pred[6400,2560]{1,0:T(32,128)(4,1)} %iota_compare_fusion, bf16[1024,256]{1,0:T(8,128)(2,1)S(1)} %copy-done.4, bf16[1024,256]{1,0:T(8,128)(2,1)S(1)} %fusion.64), kind=kOutput, calls=%fused_computation.24 | convolution fusion | flops 6714621952 | bytes 17432576 | tf_op jit(solution)/shard_map/dot_general | solution.py:125
  181.1 8.1 %fusion.26 = bf16[6400,256]{1,0:T(8,128)(2,1)} fusion(bf16[6400,256]{1,0:T(8,128)(2,1)} %fusion.23, pred[6400,2560]{1,0:T(32,128)(4,1)} %iota_compare_fusion, bf16[512,256]{1,0:T(8,128)(2,1)S(1)} %collective-permute-done.5, bf16[512,256]{1,0:T(8,128)(2,1)} %collective-permute-done.4, bf16[512,256]{1,0:T(8,128)(2,1)} %collective-permute-done.3, ...), kind=kOutput, calls=%fused_computation.25 | convolution fusion | flops 1955266560 | bytes 12189696 | tf_op jit(solution)/shard_map/dot_general | solution.py:130
  189.2 4.6 %all-to-all-start.2 = ((bf16[8,800,256]{2,1,0:T(8,128)(2,1)}), bf16[8,800,256]{2,1,0:T(8,128)(2,1)}, u32[]{:S(2)}, u32[]{:S(2)}) async-start(bf16[8,800,256]{2,1,0:T(8,128)(2,1)} %bitcast.94), calls=%async_computation.2 | async-start | bytes 6553600 | tf_op jit(solution)/shard_map/all_to_all | solution.py:136
  193.8 2.6 fusion.31
  196.5 0.3 all-gather.3.cloned.1.call-start
  197.0 32.0 %reduce-scatter.2.cloned.1.call-done = f32[2,256,256]{2,1,0:T(8,128)} async-done(((f32[8,256,256]{2,1,0:T(8,128)}), f32[2,256,256]{2,1,0:T(8,128)}) %reduce-scatter.2.cloned.1.call-update) | async-done | bytes 524304 | tf_op jit(solution)/shard_map/reduce_scatter | solution.py:138
  229.0 1.8 convert_element_type.137
  230.8 58.1 %all-to-all-done.2 = bf16[8,800,256]{2,1,0:T(8,128)(2,1)} async-done(((bf16[8,800,256]{2,1,0:T(8,128)(2,1)}), bf16[8,800,256]{2,1,0:T(8,128)(2,1)}, u32[]{:S(2)}, u32[]{:S(2)}) %all-to-all-start.2) | async-done | bytes 3276832 | tf_op jit(solution)/shard_map/all_to_all | solution.py:136
  288.9 5.6 %fusion.2 = f32[1024,256]{1,0:T(8,128)S(1)} fusion(bf16[6400,256]{1,0:T(8,128)(2,1)} %bitcast.12, s32[6400]{0:T(1024)S(1)} %eq.107, s32[1024]{0:T(1024)S(1)} %iota_add_fusion), kind=kOutput, calls=%fused_computation.5 | convolution fusion | flops 3361996800 | bytes 4355072 | tf_op jit(solution)/shard_map/dot_general | solution.py:34
  294.6 6.5 %fusion.6 = f32[1024,256]{1,0:T(8,128)} fusion(bf16[6400,256]{1,0:T(8,128)(2,1)} %bitcast.12, s32[6400]{0:T(1024)S(1)} %eq.107, s32[1024]{0:T(1024)S(1)} %iota_add_fusion.2), kind=kOutput, calls=%fused_computation.9 | convolution fusion | flops 3361996800 | bytes 4355072 | tf_op jit(solution)/shard_map/dot_general | solution.py:34
  301.1 0.5 collective-permute-start.6
  301.6 6.4 %fusion.57 = bf16[1024,256]{1,0:T(8,128)(2,1)} fusion(f32[1024,256]{1,0:T(8,128)S(1)} %collective-permute-done.7, bf16[6400,256]{1,0:T(8,128)(2,1)} %bitcast.12, s32[6400]{0:T(1024)S(1)} %eq.107, s32[1024]{0:T(1024)S(1)} %iota_add_fusion.1), kind=kOutput, calls=%fused_computation.56 | convolution fusion | flops 3362521088 | bytes 4879360 | tf_op jit(solution)/shard_map/dot_general | solution.py:34
  308.0 14.2 %collective-permute-done.8 = bf16[1024,256]{1,0:T(8,128)(2,1)} collective-permute-done((bf16[1024,256]{1,0:T(8,128)(2,1)}, bf16[1024,256]{1,0:T(8,128)(2,1)}, u32[]{:S(2)}, u32[]{:S(2)}) %collective-permute-start.8) | collective-permute-done | bytes 524320 | tf_op jit(solution)/shard_map/ppermute | solution.py:43
  322.1 7.0 %fusion.54 = f32[1024,256]{1,0:T(8,128)} fusion(f32[1024,256]{1,0:T(8,128)S(1)} %collective-permute-done.6, bf16[6400,256]{1,0:T(8,128)(2,1)} %bitcast.12, s32[6400]{0:T(1024)S(1)} %eq.107, s32[1024]{0:T(1024)S(1)} %iota_add_fusion.3, bf16[1024,256]{1,0:T(8,128)(2,1)} %collective-permute-done.8), kind=kOutput, calls=%fused_computation.55 | convolution fusion | flops 3362783232 | bytes 5927936 | tf_op jit(solution)/shard_map/dot_general | solution.py:34
  329.1 2.7 convert_reduce_fusion
  (53 shorter events, 1.6 us)
Async XLA Ops:
  7.2 29.2 %copy-start = (bf16[4096,256]{1,0:T(8,128)(2,1)S(1)}, bf16[4096,256]{1,0:T(8,128)(2,1)}, u32[]{:S(2)}) copy-start(bf16[4096,256]{1,0:T(8,128)(2,1)} %param.6) | copy-start | bytes 6291460
  55.0 4.8 %copy-start.5 = (s32[1024]{0:T(1024)S(1)}, s32[1024]{0:T(1024)}, u32[]{:S(2)}) copy-start(s32[1024]{0:T(1024)} %param.9) | copy-start | bytes 12292
  55.0 77.1 %all-to-all-start.1 = ((bf16[8,800,256]{2,1,0:T(8,128)(2,1)}), bf16[8,800,256]{2,1,0:T(8,128)(2,1)}, u32[]{:S(2)}, u32[]{:S(2)}) async-start(bf16[8,800,256]{2,1,0:T(8,128)(2,1)} %bitcast.93), calls=%async_computation.1 | async-start | bytes 6553600 | tf_op jit(solution)/shard_map/all_to_all | solution.py:74
  140.9 18.9 %collective-permute-start = (bf16[512,256]{1,0:T(8,128)(2,1)}, bf16[512,256]{1,0:T(8,128)(2,1)}, u32[]{:S(2)}, u32[]{:S(2)}) collective-permute-start(bf16[512,256]{1,0:T(8,128)(2,1)} %slice.37), channel_id=1, source_target_pairs={{0,1},{1,0},{2,3},{3,2},{4,5},{5,4},{6,7},{7,6},{8,9},{9,8},{10,11... | collective-permute-start | bytes 786440 | tf_op jit(solution)/shard_map/ppermute | solution.py:85
  140.9 10.0 %collective-permute-start.2 = (bf16[512,256]{1,0:T(8,128)(2,1)}, bf16[512,256]{1,0:T(8,128)(2,1)}, u32[]{:S(2)}, u32[]{:S(2)}) collective-permute-start(bf16[512,256]{1,0:T(8,128)(2,1)} %slice.37), channel_id=1, source_target_pairs={{0,3},{1,2},{2,1},{3,0},{4,7},{5,6},{6,5},{7,4},{8,11},{9,10},{10,... | collective-permute-start | bytes 786440 | tf_op jit(solution)/shard_map/ppermute | solution.py:85
  142.5 12.9 %collective-permute-start.1 = (bf16[512,256]{1,0:T(8,128)(2,1)}, bf16[512,256]{1,0:T(8,128)(2,1)}, u32[]{:S(2)}, u32[]{:S(2)}) collective-permute-start(bf16[512,256]{1,0:T(8,128)(2,1)} %slice.37), channel_id=1, source_target_pairs={{0,2},{1,3},{2,0},{3,1},{4,6},{5,7},{6,4},{7,5},{8,10},{9,11},{10,... | collective-permute-start | bytes 786440 | tf_op jit(solution)/shard_map/ppermute | solution.py:85
  148.7 12.9 %copy-start.2 = (bf16[1024,256]{1,0:T(8,128)(2,1)}, bf16[1024,256]{1,0:T(8,128)(2,1)S(1)}, u32[]{:S(2)}) copy-start(bf16[1024,256]{1,0:T(8,128)(2,1)S(1)} %get-tuple-element.9) | copy-start | bytes 1572868
  149.5 3.2 copy-start.6
  153.9 27.2 %collective-permute-start.5 = (bf16[512,256]{1,0:T(8,128)(2,1)}, bf16[512,256]{1,0:T(8,128)(2,1)S(1)}, u32[]{:S(2)}, u32[]{:S(2)}) collective-permute-start(bf16[512,256]{1,0:T(8,128)(2,1)} %convolution_convert_fusion.1), channel_id=1, source_target_pairs={{0,3},{1,2},{2,1},{3,0},{4,7},{5,6},{6,5},{7,4},{8,11},{9,10},{10,... | collective-permute-start | bytes 786440 | tf_op jit(solution)/shard_map/ppermute | solution.py:113
  158.4 22.7 %collective-permute-start.4 = (bf16[512,256]{1,0:T(8,128)(2,1)}, bf16[512,256]{1,0:T(8,128)(2,1)}, u32[]{:S(2)}, u32[]{:S(2)}) collective-permute-start(bf16[512,256]{1,0:T(8,128)(2,1)} %convolution_convert_fusion.2), channel_id=1, source_target_pairs={{0,2},{1,3},{2,0},{3,1},{4,6},{5,7},{6,4},{7,5},{8,10},{9,11},{10,... | collective-permute-start | bytes 786440 | tf_op jit(solution)/shard_map/ppermute | solution.py:113
  162.8 18.3 %collective-permute-start.3 = (bf16[512,256]{1,0:T(8,128)(2,1)}, bf16[512,256]{1,0:T(8,128)(2,1)}, u32[]{:S(2)}, u32[]{:S(2)}) collective-permute-start(bf16[512,256]{1,0:T(8,128)(2,1)} %convolution_convert_fusion.3), channel_id=1, source_target_pairs={{0,1},{1,0},{2,3},{3,2},{4,5},{5,4},{6,7},{7,6},{8,9},{9,8},{10,11... | collective-permute-start | bytes 786440 | tf_op jit(solution)/shard_map/ppermute | solution.py:113
  167.2 2.6 copy-start.4
  169.8 11.3 %copy-start.3 = (bf16[1024,256]{1,0:T(8,128)(2,1)S(1)}, bf16[1024,256]{1,0:T(8,128)(2,1)}, u32[]{:S(2)}) copy-start(bf16[1024,256]{1,0:T(8,128)(2,1)} %copy-done.2) | copy-start | bytes 1572868
  189.2 4.6 %copy-start.1 = (bf16[1024,256]{0,1:T(8,128)(2,1)S(1)}, bf16[1024,256]{0,1:T(8,128)(2,1)}, u32[]{:S(2)}) copy-start(bf16[1024,256]{0,1:T(8,128)(2,1)} %copy.15) | copy-start | bytes 1572868
  189.2 99.7 %all-to-all-start.2 = ((bf16[8,800,256]{2,1,0:T(8,128)(2,1)}), bf16[8,800,256]{2,1,0:T(8,128)(2,1)}, u32[]{:S(2)}, u32[]{:S(2)}) async-start(bf16[8,800,256]{2,1,0:T(8,128)(2,1)} %bitcast.94), calls=%async_computation.2 | async-start | bytes 6553600 | tf_op jit(solution)/shard_map/all_to_all | solution.py:136
  193.8 35.2 %reduce-scatter.2.cloned.1.call-start = ((), (), s32[]{:S(2)}) async-start(), calls=%async_computation.4 | async-start | bytes 2621440 | tf_op jit(solution)/shard_map/reduce_scatter | solution.py:138
  196.5 132.7 %all-gather.3.cloned.1.call-start = ((), (), s32[]{:S(2)}) async-start(), calls=%async_computation.5 | async-start | bytes 2359296 | tf_op jit(solution)/shard_map/all_gather | solution.py:139
  294.5 7.1 %collective-permute-start.7 = (f32[1024,256]{1,0:T(8,128)S(1)}, f32[1024,256]{1,0:T(8,128)S(1)}, u32[]{:S(2)}, u32[]{:S(2)}) collective-permute-start(f32[1024,256]{1,0:T(8,128)S(1)} %fusion.2), channel_id=1, source_target_pairs={{0,1},{1,0},{2,3},{3,2},{4,5},{5,4},{6,7},{7,6},{8,9},{9,8},{10,11... | collective-permute-start | bytes 3145736 | tf_op jit(solution)/shard_map/ppermute | solution.py:39
  301.1 6.9 %collective-permute-start.6 = (f32[1024,256]{1,0:T(8,128)}, f32[1024,256]{1,0:T(8,128)S(1)}, u32[]{:S(2)}, u32[]{:S(2)}) collective-permute-start(f32[1024,256]{1,0:T(8,128)} %fusion.6), channel_id=1, source_target_pairs={{0,1},{1,0},{2,3},{3,2},{4,5},{5,4},{6,7},{7,6},{8,9},{9,8},{10,11... | collective-permute-start | bytes 3145736 | tf_op jit(solution)/shard_map/ppermute | solution.py:39
  308.0 14.2 %collective-permute-start.8 = (bf16[1024,256]{1,0:T(8,128)(2,1)}, bf16[1024,256]{1,0:T(8,128)(2,1)}, u32[]{:S(2)}, u32[]{:S(2)}) collective-permute-start(bf16[1024,256]{1,0:T(8,128)(2,1)} %fusion.57), channel_id=1, source_target_pairs={{0,2},{1,3},{2,0},{3,1},{4,6},{5,7},{6,4},{7,5},{8,10},{9,11},{10,... | collective-permute-start | bytes 1572872 | tf_op jit(solution)/shard_map/ppermute | solution.py:43
Sparse Core Ops, SparseCore 0:
  197.1 31.8 reduce-scatter.1
  231.3 62.5 all-gather.2
where the time goes:
time: 345 us; the launch traced here: 339 us
  waiting for transfers between devices  163 us (47%)
  matrix products  78.6 us (23%)
  local copies, waits for them, and re-layouts  32.9 us (10%)
  other arithmetic  21.2 us (6%)
  between operations  15 us (4%)
  starting transfers between devices  14.7 us (4%)
  blocking collectives  13.7 us (4%)
    all_to_all x1, waiting for transfers between devices, shards(): lax.all_to_all(outgoing, 'owner', split_axis=0, concat_axis=0, tiled=True)  58.1 us
    all_to_all x1, waiting for transfers between devices, shards(): lax.all_to_all(found_rows, 'owner', split_axis=0, concat_axis=0, tiled=True)  57.9 us
    reduce_scatter x1, waiting for transfers between devices, shards(): lax.psum_scatter(rel_term, 'blk', scatter_dimension=0, tiled=True)  32 us
    dot_general x4, matrix products, block(): return jnp.dot(landing, grads, preferred_element_type=jnp.float32)  25.5 us
    gather x1, local copies, waits for them, and re-layouts, shards(): found_rows = entity_table.at[asked_rows].get(mode='promise_in_bounds')  18.6 us
    eq x1, other arithmetic, shards(): packing = (slots[:, None] == target[None, :]).astype(jnp.bfloat16)  14.4 us
    ppermute x1, waiting for transfers between devices, group_sums(): arrived.append(lax.ppermute(total.astype(jnp.bfloat16), 'blk', route))  14.2 us
    all_to_all x1, blocking collectives, shards(): lax.all_to_all(requests, 'owner', split_axis=0, concat_axis=0, tiled=True)  13.7 us
  transfers between devices with their start and end apart: 13, of which 5 were waited for; matrix products, arithmetic and copies ran while one was open for 23% of the time, Pallas kernels for 0%

commit v1 on v0

--- a/solution.py
+++ b/solution.py
@@ -37,7 +37,7 @@
     for step in range(1, pairs + 1):
         target = (pair + step) % pairs
         other = lax.ppermute(block(2 * target + 1 - core), "blk", swap)
-        total = block(2 * target + core) + other
+        total = lax.optimization_barrier(block(2 * target + core)) + other
         if step < pairs:
             route = [(i, (i + 2 * step) % members) for i in range(members)]
             arrived.append(lax.ppermute(total.astype(jnp.bfloat16), "blk", route))
@@ -120,7 +120,17 @@
     rel_term = lax.dot_general(
         spread_heads, partner_low, contract_rows, preferred_element_type=jnp.float32
     )
-    rel_term = rel_term.reshape(relation_count, feature_count, feature_count)
+    shares = rel_term.reshape(cycle_count, -1, feature_count)
+    me = lax.axis_index("blk")
+    share = lax.dynamic_index_in_dim(shares, me, keepdims=False)
+    sent = [
+        lax.dynamic_index_in_dim(shares, jnp.bitwise_xor(me, step), keepdims=False)
+        for step in range(1, cycle_count)
+    ]
+    for step in range(1, cycle_count):
+        part = lax.ppermute(sent[step - 1].astype(jnp.bfloat16), "blk", routes[step])
+        share = share + part.astype(jnp.float32)
+    relation_rows = share.astype(jnp.bfloat16).reshape(owner_count, -1, feature_count)
     triple_grads = jnp.concatenate([head_grad, tail_grad], axis=0).astype(jnp.bfloat16)
     outgoing = jnp.dot(
         packing[:, : 2 * triple_count], triple_grads, preferred_element_type=jnp.float32
@@ -133,11 +143,13 @@
         preferred_element_type=jnp.float32,
     ).astype(jnp.bfloat16)
     outgoing = outgoing.reshape(owner_count, capacity, feature_count)
+    outgoing = jnp.concatenate([outgoing, relation_rows], axis=1)
     returned = lax.all_to_all(outgoing, "owner", split_axis=0, concat_axis=0, tiled=True)
-    ent_grad = group_sums(asked_rows.reshape(-1), returned.reshape(-1, feature_count), entity_rows)
-    summed_group = lax.psum_scatter(rel_term, "blk", scatter_dimension=0, tiled=True)
-    gathered = lax.all_gather(summed_group.astype(jnp.bfloat16), "owner")
-    rel_grad = jnp.sum(gathered.astype(jnp.float32), axis=0)
+    summed_rows = jnp.sum(returned[:, capacity:].astype(jnp.float32), axis=0)
+    rel_grad = lax.all_gather(summed_rows, "owner", tiled=True)
+    rel_grad = rel_grad.reshape(relation_count // cycle_count, feature_count, feature_count)
+    rows = jnp.pad(asked_rows, ((0, 0), (0, relation_rows.shape[1])), constant_values=-1)
+    ent_grad = group_sums(rows.reshape(-1), returned.reshape(-1, feature_count), entity_rows)
     return (ent_grad, rel_grad)
 
 

time: 345 us -> 339 us (0.983)
  blocking collectives: 13.7 us -> 45.5 us
  waiting for transfers between devices: 163 us -> 145 us
  matrix products: 78.6 us -> 64.7 us
  between operations: 15 us -> 1.46 us
  local copies, waits for them, and re-layouts: 32.9 us -> 37.9 us
    reduce_scatter x1 -> x0, waiting for transfers between devices: 32 us -> none  [shards(): lax.psum_scatter(rel_term, 'blk', scatter_dimension=0, tiled=True)]
    all_gather x0 -> x1, blocking collectives: none -> 31.8 us  [shards(): rel_grad = lax.all_gather(summed_rows, 'owner', tiled=True)]
    all_to_all x1, waiting for transfers between devices: 58.1 us -> 76.7 us  [shards(): lax.all_to_all(outgoing, 'owner', split_axis=0, concat_axis=0, tiled=True)]
    dot_general x4, matrix products: 25.5 us -> 18.5 us  [block(): return jnp.dot(landing, grads, preferred_element_type=jnp.float32)]
    ppermute x1, waiting for transfers between devices: 14.2 us -> 7.75 us  [group_sums(): arrived.append(lax.ppermute(total.astype(jnp.bfloat16), 'blk', route))]
  transfers between devices with their start and end apart: 13 -> 14, of which waited for: 5 -> 4; matrix products, arithmetic and copies ran while one was open for 23% -> 18% of each run, Pallas kernels for 0% -> 0%
where the time goes in v1:
time: 339 us; the launch traced here: 332 us
  waiting for transfers between devices  145 us (43%)
  matrix products  64.7 us (19%)
  blocking collectives  45.5 us (13%)
  local copies, waits for them, and re-layouts  37.9 us (11%)
  other arithmetic  21.7 us (6%)
  starting transfers between devices  16.2 us (5%)
    all_to_all x1, waiting for transfers between devices, shards(): lax.all_to_all(outgoing, 'owner', split_axis=0, concat_axis=0, tiled=True)  76.7 us
    all_to_all x1, waiting for transfers between devices, shards(): lax.all_to_all(found_rows, 'owner', split_axis=0, concat_axis=0, tiled=True)  57.8 us
    all_gather x1, blocking collectives, shards(): rel_grad = lax.all_gather(summed_rows, 'owner', tiled=True)  31.8 us
    gather x1, local copies, waits for them, and re-layouts, shards(): found_rows = entity_table.at[asked_rows].get(mode='promise_in_bounds')  18.6 us
    dot_general x4, matrix products, block(): return jnp.dot(landing, grads, preferred_element_type=jnp.float32)  18.5 us
    eq x1, other arithmetic, shards(): packing = (slots[:, None] == target[None, :]).astype(jnp.bfloat16)  14.4 us
    all_to_all x1, blocking collectives, shards(): lax.all_to_all(requests, 'owner', split_axis=0, concat_axis=0, tiled=True)  13.7 us
    dot_general x1, matrix products, shards(): jnp.dot(packing, digits, preferred_element_type=jnp.float32)  11.4 us
  transfers between devices with their start and end apart: 14, of which 4 were waited for; matrix products, arithmetic and copies ran while one was open for 18% of the time, Pallas kernels for 0%

profile of v1, /device:TPU:0, one launch (start us, length us, event | category | flops | bytes accessed | tf_op | source)
XLA Modules:
  0.0 332.4 jit_solution(16634465113289708525)
XLA Ops:
  0.6 0.8 constant_dynamic-update-slice_fusion.2
  1.5 0.7 constant_dynamic-update-slice_fusion.1
  2.2 0.7 constant_dynamic-update-slice_fusion
  2.9 0.8 fusion.85
  4.3 11.4 %convolution_convert_fusion = s32[6400,2]{0,1:T(2,128)S(1)} fusion(s32[2560]{0:T(1024)S(1)} %fusion.69, bf16[2560,1]{0,1:T(2,128)(2,1)S(1)} %fusion.76, bf16[2560,1]{0,1:T(2,128)(2,1)S(1)} %get-tuple-element.4), kind=kOutput, calls=%fused_computation.26 | convolution fusion | flops 81953280 | bytes 71680 | tf_op jit(solution)/shard_map/dot_general | solution.py:69
  15.9 13.7 %all_to_all.22 = s32[8,1,800]{2,1,0:T(1,128)S(1)} all-to-all(s32[8,1,800]{2,1,0:T(1,128)S(1)} %add.313), channel_id=1, replica_groups=mesh['owner'=8,'blk'=4] {'owner'}, dimensions={0} | all-to-all | bytes 51200 | tf_op jit(solution)/shard_map/all_to_all | solution.py:71
  29.7 0.6 copy-done.6
  30.5 18.6 %gather_fusion = bf16[6400,256]{1,0:T(8,128)(2,1)} fusion(bf16[4096,256]{1,0:T(8,128)(2,1)S(1)} %copy-done, s32[7168]{0:T(1024)S(1)} %pad_clamp_fusion), kind=kCustom, calls=%fused_computation | custom fusion | bytes 6579200 | tf_op jit(solution)/shard_map/gather | solution.py:72
  49.1 3.8 %all-to-all-start.1 = ((bf16[8,800,256]{2,1,0:T(8,128)(2,1)}), bf16[8,800,256]{2,1,0:T(8,128)(2,1)S(1)}, u32[]{:S(2)}, u32[]{:S(2)}) async-start(bf16[8,800,256]{2,1,0:T(8,128)(2,1)} %bitcast.110), calls=%async_computation.1 | async-start | bytes 6553600 | tf_op jit(solution)/shard_map/all_to_all | solution.py:74
  52.9 14.4 %iota_compare_fusion = pred[6400,2560]{1,0:T(32,128)(4,1)} fusion(s32[2560]{0:T(1024)S(1)} %fusion.69), kind=kLoop, calls=%fused_computation.2 | loop fusion | flops 16384000 | bytes 16394240 | tf_op jit(solution)/shard_map/eq | solution.py:67
  67.3 57.8 %all-to-all-done.1 = bf16[8,800,256]{2,1,0:T(8,128)(2,1)S(1)} async-done(((bf16[8,800,256]{2,1,0:T(8,128)(2,1)}), bf16[8,800,256]{2,1,0:T(8,128)(2,1)S(1)}, u32[]{:S(2)}, u32[]{:S(2)}) %all-to-all-start.1) | async-done | bytes 3276832 | tf_op jit(solution)/shard_map/all_to_all | solution.py:74
  125.2 8.6 %gather_fusion.1 = bf16[2560,256]{1,0:T(8,128)(2,1)} fusion(bf16[6400,256]{1,0:T(8,128)(2,1)S(1)} %bitcast.109, s32[3072]{0:T(1024)S(1)} %pad_clamp_fusion.1), kind=kCustom, calls=%fused_computation.1 | custom fusion | bytes 2631680 | tf_op jit(solution)/shard_map/gather | solution.py:78
  133.8 1.7 slice.41
  135.5 1.6 collective-permute-start.2
  137.6 1.1 slice.39
  138.9 2.3 broadcast_multiply_fusion
  141.2 1.4 fusion.46
  142.6 0.8 multiply_convert_fusion.3
  144.1 0.8 multiply_convert_fusion
  144.8 1.2 convolution_convert_fusion.1
  146.1 1.8 collective-permute-start.5
  147.8 2.7 collective-permute-done.1
  150.5 1.7 multiply_convert_fusion.1
  152.2 1.2 convolution_convert_fusion.2
  153.5 1.5 collective-permute-start.4
  155.0 0.7 multiply_convert_fusion.2
  155.7 1.2 convolution_convert_fusion.3
  157.4 1.4 fusion.88
  159.2 1.0 copy.17
  160.2 3.6 %fusion.54 = f32[4,512,256]{2,1,0:T(8,128)S(1)} fusion(bf16[4,512,1024]{2,1,0:T(8,128)(2,1)} %bitcast.111, bf16[1024,256]{1,0:T(8,128)(2,1)S(1)} %fusion.38), kind=kOutput, calls=%fused_computation.67 | convolution fusion | flops 1073741824 | bytes 6815744 | tf_op jit(solution)/shard_map/dot_general | solution.py:120
  164.6 1.4 fusion.39
  166.0 1.6 collective-permute-start.7
  167.6 11.2 %fusion.23 = bf16[6400,256]{1,0:T(8,128)(2,1)} fusion(pred[6400,2560]{1,0:T(32,128)(4,1)} %iota_compare_fusion, bf16[1024,256]{1,0:T(8,128)(2,1)S(1)} %fusion.47, bf16[1024,256]{1,0:T(8,128)(2,1)S(1)} %fusion.39), kind=kOutput, calls=%fused_computation.24 | convolution fusion | flops 6714621952 | bytes 17432576 | tf_op jit(solution)/shard_map/dot_general | solution.py:135
  179.0 6.6 %fusion.26 = bf16[6400,256]{1,0:T(8,128)(2,1)S(1)} fusion(bf16[6400,256]{1,0:T(8,128)(2,1)} %fusion.23, pred[6400,2560]{1,0:T(32,128)(4,1)} %iota_compare_fusion, bf16[512,256]{1,0:T(8,128)(2,1)} %collective-permute-done.5, bf16[512,256]{1,0:T(8,128)(2,1)} %collective-permute-done.4, bf16[512,256]{1,0:T(8,128)(2,1)} %collective-permute-done.3, ...), kind=kOutput, calls=%fused_computation.25 | convolution fusion | flops 1955266560 | bytes 12189696 | tf_op jit(solution)/shard_map/dot_general | solution.py:140
  185.6 2.0 pad_maximum_fusion
  187.6 3.9 %all-to-all-start.2 = ((bf16[8,864,256]{2,1,0:T(8,128)(2,1)}), bf16[8,864,256]{2,1,0:T(8,128)(2,1)S(1)}, u32[]{:S(2)}, u32[]{:S(2)}) async-start(bf16[8,864,256]{2,1,0:T(8,128)(2,1)} %pad_maximum_fusion), calls=%async_computation.2 | async-start | bytes 7077888 | tf_op jit(solution)/shard_map/all_to_all | solution.py:147
  191.6 0.8 copy.31
  192.4 0.6 pad.4
  193.0 1.4 eq.107
  194.4 76.7 %all-to-all-done.2 = bf16[8,864,256]{2,1,0:T(8,128)(2,1)S(1)} async-done(((bf16[8,864,256]{2,1,0:T(8,128)(2,1)}), bf16[8,864,256]{2,1,0:T(8,128)(2,1)S(1)}, u32[]{:S(2)}, u32[]{:S(2)}) %all-to-all-start.2) | async-done | bytes 3538976 | tf_op jit(solution)/shard_map/all_to_all | solution.py:147
  271.1 4.7 %fusion.2 = f32[1024,256]{1,0:T(8,128)S(1)} fusion(bf16[6912,256]{1,0:T(8,128)(2,1)S(1)} %bitcast.112, s32[6912]{0:T(1024)} %eq.107, s32[1024]{0:T(1024)S(1)} %iota_add_fusion), kind=kOutput, calls=%fused_computation.5 | convolution fusion | flops 3630956544 | bytes 4619264 | tf_op jit(solution)/shard_map/dot_general | solution.py:34
  275.8 3.9 %fusion.4 = f32[1024,256]{1,0:T(8,128)S(1)} fusion(bf16[6912,256]{1,0:T(8,128)(2,1)S(1)} %bitcast.113, s32[6912]{0:T(1024)S(1)} %copy-done.7, s32[1024]{0:T(1024)S(1)} %iota_add_fusion.1), kind=kOutput, calls=%fused_computation.7 | convolution fusion | flops 3630956544 | bytes 4619264 | tf_op jit(solution)/shard_map/dot_general | solution.py:34
  279.9 31.8 %all_gather.3 = f32[512,256]{1,0:T(8,128)S(1)} all-gather(f32[64,256]{1,0:T(8,128)S(1)} %convert_reduce_fusion), channel_id=1, replica_groups=mesh['owner'=8,'blk'=4] {'owner'}, dimensions={0}, use_global_device_ids=true | all-gather | bytes 589824 | tf_op jit(solution)/shard_map/all_gather | solution.py:149
  311.6 3.9 %fusion.6 = f32[1024,256]{1,0:T(8,128)S(1)} fusion(bf16[6912,256]{1,0:T(8,128)(2,1)S(1)} %bitcast.114, s32[6912]{0:T(1024)S(1)} %copy-done.7, s32[1024]{0:T(1024)S(1)} %iota_add_fusion.2), kind=kOutput, calls=%fused_computation.9 | convolution fusion | flops 3630956544 | bytes 4619264 | tf_op jit(solution)/shard_map/dot_general | solution.py:34
  316.4 6.0 %fusion.8 = f32[1024,256]{1,0:T(8,128)S(1)} fusion(bf16[6912,256]{1,0:T(8,128)(2,1)} %bitcast.115, s32[6912]{0:T(1024)S(1)} %copy-done.7, s32[1024]{0:T(1024)S(1)} %iota_add_fusion.3), kind=kOutput, calls=%fused_computation.11 | convolution fusion | flops 3630956544 | bytes 4619264 | tf_op jit(solution)/shard_map/dot_general | solution.py:34
  322.4 7.8 %collective-permute-done.11 = bf16[1024,256]{1,0:T(8,128)(2,1)S(1)} collective-permute-done((bf16[1024,256]{1,0:T(8,128)(2,1)S(1)}, bf16[1024,256]{1,0:T(8,128)(2,1)S(1)}, u32[]{:S(2)}, u32[]{:S(2)}) %collective-permute-start.11) | collective-permute-done | bytes 524320 | tf_op jit(solution)/shard_map/ppermute | solution.py:43
  330.2 1.1 convert_add_fusion
  331.3 0.8 copy.36
  (71 shorter events, 5.3 us)
Async XLA Ops:
  0.6 29.9 %copy-start = (bf16[4096,256]{1,0:T(8,128)(2,1)S(1)}, bf16[4096,256]{1,0:T(8,128)(2,1)}, u32[]{:S(2)}) copy-start(bf16[4096,256]{1,0:T(8,128)(2,1)} %param.6) | copy-start | bytes 6291460
  29.7 0.6 copy-start.6
  49.1 3.8 %copy-start.8 = (s32[1024]{0:T(1024)S(1)}, s32[1024]{0:T(1024)}, u32[]{:S(2)}) copy-start(s32[1024]{0:T(1024)} %param.9) | copy-start | bytes 12292
  49.1 76.1 %all-to-all-start.1 = ((bf16[8,800,256]{2,1,0:T(8,128)(2,1)}), bf16[8,800,256]{2,1,0:T(8,128)(2,1)S(1)}, u32[]{:S(2)}, u32[]{:S(2)}) async-start(bf16[8,800,256]{2,1,0:T(8,128)(2,1)} %bitcast.110), calls=%async_computation.1 | async-start | bytes 6553600 | tf_op jit(solution)/shard_map/all_to_all | solution.py:74
  135.4 5.7 %copy-start.3 = (bf16[2560,256]{1,0:T(8,128)(2,1)S(1)}, bf16[2560,256]{1,0:T(8,128)(2,1)}, u32[]{:S(2)}) copy-start(bf16[2560,256]{1,0:T(8,128)(2,1)} %gather_fusion.1) | copy-start | bytes 3932164
  135.5 19.5 %collective-permute-start = (bf16[512,256]{1,0:T(8,128)(2,1)}, bf16[512,256]{1,0:T(8,128)(2,1)S(1)}, u32[]{:S(2)}, u32[]{:S(2)}) collective-permute-start(bf16[512,256]{1,0:T(8,128)(2,1)} %slice.41), channel_id=1, source_target_pairs={{0,1},{1,0},{2,3},{3,2},{4,5},{5,4},{6,7},{7,6},{8,9},{9,8},{10,11... | collective-permute-start | bytes 786440 | tf_op jit(solution)/shard_map/ppermute | solution.py:85
  135.5 8.6 %collective-permute-start.2 = (bf16[512,256]{1,0:T(8,128)(2,1)}, bf16[512,256]{1,0:T(8,128)(2,1)S(1)}, u32[]{:S(2)}, u32[]{:S(2)}) collective-permute-start(bf16[512,256]{1,0:T(8,128)(2,1)} %slice.41), channel_id=1, source_target_pairs={{0,3},{1,2},{2,1},{3,0},{4,7},{5,6},{6,5},{7,4},{8,11},{9,10},{10,... | collective-permute-start | bytes 786440 | tf_op jit(solution)/shard_map/ppermute | solution.py:85
  137.1 13.5 %collective-permute-start.1 = (bf16[512,256]{1,0:T(8,128)(2,1)}, bf16[512,256]{1,0:T(8,128)(2,1)}, u32[]{:S(2)}, u32[]{:S(2)}) collective-permute-start(bf16[512,256]{1,0:T(8,128)(2,1)} %slice.41), channel_id=1, source_target_pairs={{0,2},{1,3},{2,0},{3,1},{4,6},{5,7},{6,4},{7,5},{8,10},{9,11},{10,... | collective-permute-start | bytes 786440 | tf_op jit(solution)/shard_map/ppermute | solution.py:85
  138.9 2.3 copy-start.9
  142.6 13.1 %copy-start.4 = (bf16[1024,256]{1,0:T(8,128)(2,1)}, bf16[1024,256]{1,0:T(8,128)(2,1)S(1)}, u32[]{:S(2)}) copy-start(bf16[1024,256]{1,0:T(8,128)(2,1)S(1)} %get-tuple-element.12) | copy-start | bytes 1572868
  143.4 1.4 copy-start.11
  146.1 32.9 %collective-permute-start.5 = (bf16[512,256]{1,0:T(8,128)(2,1)}, bf16[512,256]{1,0:T(8,128)(2,1)}, u32[]{:S(2)}, u32[]{:S(2)}) collective-permute-start(bf16[512,256]{1,0:T(8,128)(2,1)} %convolution_convert_fusion.1), channel_id=1, source_target_pairs={{0,3},{1,2},{2,1},{3,0},{4,7},{5,6},{6,5},{7,4},{8,11},{9,10},{10,... | collective-permute-start | bytes 786440 | tf_op jit(solution)/shard_map/ppermute | solution.py:113
  153.5 25.5 %collective-permute-start.4 = (bf16[512,256]{1,0:T(8,128)(2,1)}, bf16[512,256]{1,0:T(8,128)(2,1)}, u32[]{:S(2)}, u32[]{:S(2)}) collective-permute-start(bf16[512,256]{1,0:T(8,128)(2,1)} %convolution_convert_fusion.2), channel_id=1, source_target_pairs={{0,2},{1,3},{2,0},{3,1},{4,6},{5,7},{6,4},{7,5},{8,10},{9,11},{10,... | collective-permute-start | bytes 786440 | tf_op jit(solution)/shard_map/ppermute | solution.py:113
  156.9 22.0 %collective-permute-start.3 = (bf16[512,256]{1,0:T(8,128)(2,1)}, bf16[512,256]{1,0:T(8,128)(2,1)}, u32[]{:S(2)}, u32[]{:S(2)}) collective-permute-start(bf16[512,256]{1,0:T(8,128)(2,1)} %convolution_convert_fusion.3), channel_id=1, source_target_pairs={{0,1},{1,0},{2,3},{3,2},{4,5},{5,4},{6,7},{7,6},{8,9},{9,8},{10,11... | collective-permute-start | bytes 786440 | tf_op jit(solution)/shard_map/ppermute | solution.py:113
  160.2 4.4 %copy-start.5 = (bf16[1024,256]{0,1:T(8,128)(2,1)S(1)}, bf16[1024,256]{0,1:T(8,128)(2,1)}, u32[]{:S(2)}) copy-start(bf16[1024,256]{0,1:T(8,128)(2,1)} %copy.17) | copy-start | bytes 1572868
  160.2 4.4 %copy-start.10 = (bf16[8,256,256]{2,1,0:T(8,128)(2,1)S(1)}, bf16[8,256,256]{2,1,0:T(8,128)(2,1)}, u32[]{:S(2)}) copy-start(bf16[8,256,256]{2,1,0:T(8,128)(2,1)} %param.7) | copy-start | bytes 3145732
  163.9 2.1 collective-permute-start.6
  164.4 14.3 %collective-permute-start.8 = (bf16[512,256]{1,0:T(8,128)(2,1)S(1)}, bf16[512,256]{1,0:T(8,128)(2,1)S(1)}, u32[]{:S(2)}, u32[]{:S(2)}) collective-permute-start(bf16[512,256]{1,0:T(8,128)(2,1)S(1)} %get-tuple-element.9), channel_id=1, source_target_pairs={{0,3},{1,2},{2,1},{3,0},{4,7},{5,6},{6,5},{7,4},{8,11},{9,10},{10,... | collective-permute-start | bytes 786440 | tf_op jit(solution)/shard_map/ppermute | solution.py:131
  166.0 12.8 %collective-permute-start.7 = (bf16[512,256]{1,0:T(8,128)(2,1)S(1)}, bf16[512,256]{1,0:T(8,128)(2,1)S(1)}, u32[]{:S(2)}, u32[]{:S(2)}) collective-permute-start(bf16[512,256]{1,0:T(8,128)(2,1)S(1)} %get-tuple-element.10), channel_id=1, source_target_pairs={{0,2},{1,3},{2,0},{3,1},{4,6},{5,7},{6,4},{7,5},{8,10},{9,11},{10,... | collective-permute-start | bytes 786440 | tf_op jit(solution)/shard_map/ppermute | solution.py:131
  187.6 83.5 %all-to-all-start.2 = ((bf16[8,864,256]{2,1,0:T(8,128)(2,1)}), bf16[8,864,256]{2,1,0:T(8,128)(2,1)S(1)}, u32[]{:S(2)}, u32[]{:S(2)}) async-start(bf16[8,864,256]{2,1,0:T(8,128)(2,1)} %pad_maximum_fusion), calls=%async_computation.2 | async-start | bytes 7077888 | tf_op jit(solution)/shard_map/all_to_all | solution.py:147
  271.1 40.5 %copy-start.2 = (bf16[8,864,256]{2,1,0:T(8,128)(2,1)}, bf16[8,864,256]{2,1,0:T(8,128)(2,1)S(1)}, u32[]{:S(2)}) copy-start(bf16[8,864,256]{2,1,0:T(8,128)(2,1)S(1)} %all-to-all-done.2) | copy-start | bytes 10616836
  271.1 4.7 %copy-start.7 = (s32[6912]{0:T(1024)S(1)}, s32[6912]{0:T(1024)}, u32[]{:S(2)}) copy-start(s32[6912]{0:T(1024)} %eq.107) | copy-start | bytes 82948
  279.7 35.9 %collective-permute-start.10 = (f32[1024,256]{1,0:T(8,128)S(1)}, f32[1024,256]{1,0:T(8,128)S(1)}, u32[]{:S(2)}, u32[]{:S(2)}) collective-permute-start(f32[1024,256]{1,0:T(8,128)S(1)} %fusion.2), channel_id=1, source_target_pairs={{0,1},{1,0},{2,3},{3,2},{4,5},{5,4},{6,7},{7,6},{8,9},{9,8},{10,11... | collective-permute-start | bytes 3145736 | tf_op jit(solution)/shard_map/ppermute | solution.py:39
  315.5 6.9 %collective-permute-start.9 = (f32[1024,256]{1,0:T(8,128)S(1)}, f32[1024,256]{1,0:T(8,128)S(1)}, u32[]{:S(2)}, u32[]{:S(2)}) collective-permute-start(f32[1024,256]{1,0:T(8,128)S(1)} %fusion.6), channel_id=1, source_target_pairs={{0,1},{1,0},{2,3},{3,2},{4,5},{5,4},{6,7},{7,6},{8,9},{9,8},{10,11... | collective-permute-start | bytes 3145736 | tf_op jit(solution)/shard_map/ppermute | solution.py:39
  315.8 14.4 %collective-permute-start.11 = (bf16[1024,256]{1,0:T(8,128)(2,1)S(1)}, bf16[1024,256]{1,0:T(8,128)(2,1)S(1)}, u32[]{:S(2)}, u32[]{:S(2)}) collective-permute-start(bf16[1024,256]{1,0:T(8,128)(2,1)S(1)} %add_convert_fusion), channel_id=1, source_target_pairs={{0,2},{1,3},{2,0},{3,1},{4,6},{5,7},{6,4},{7,5},{8,10},{9,11},{10,... | collective-permute-start | bytes 1572872 | tf_op jit(solution)/shard_map/ppermute | solution.py:43
  316.4 15.7 %copy-start.1 = (bf16[4096,256]{1,0:T(8,128)(2,1)S(1)}, bf16[4096,256]{1,0:T(8,128)(2,1)}, u32[]{:S(2)}) copy-start(bf16[4096,256]{1,0:T(8,128)(2,1)} %param.6) | copy-start | bytes 6291460

commit v2 on v1

--- a/solution.py
+++ b/solution.py
@@ -146,7 +146,15 @@
     outgoing = jnp.concatenate([outgoing, relation_rows], axis=1)
     returned = lax.all_to_all(outgoing, "owner", split_axis=0, concat_axis=0, tiled=True)
     summed_rows = jnp.sum(returned[:, capacity:].astype(jnp.float32), axis=0)
-    rel_grad = lax.all_gather(summed_rows, "owner", tiled=True)
+    holder = lax.axis_index("owner")
+    rel_grad = jnp.zeros((owner_count, *summed_rows.shape), jnp.float32)
+    for step in range(owner_count):
+        piece = summed_rows
+        if step > 0:
+            piece = lax.ppermute(piece, "owner", [(i, i ^ step) for i in range(owner_count)])
+        rel_grad = lax.dynamic_update_index_in_dim(
+            rel_grad, piece, jnp.bitwise_xor(holder, step), 0
+        )
     rel_grad = rel_grad.reshape(relation_count // cycle_count, feature_count, feature_count)
     rows = jnp.pad(asked_rows, ((0, 0), (0, relation_rows.shape[1])), constant_values=-1)
     ent_grad = group_sums(rows.reshape(-1), returned.reshape(-1, feature_count), entity_rows)

time: 339 us -> 337 us (level); the launches traced: 332 us -> 337 us
  blocking collectives: 45.5 us -> 13.7 us
  waiting for transfers between devices: 145 us -> 159 us
  starting transfers between devices: 16.2 us -> 29.6 us
  matrix products: 64.7 us -> 74.9 us
    all_gather x1 -> x0, blocking collectives: 31.8 us -> none  [shards(): rel_grad = lax.all_gather(summed_rows, 'owner', tiled=True)]
    ppermute x0 -> x7, starting transfers between devices: none -> 13.6 us  [shards(): lax.ppermute(piece, 'owner', [(i, i ^ step) for i in range(owner_count)])]
    dot_general x1, matrix products: 11.2 us -> 23.4 us  [shards(): jnp.dot(packing[:, :2 * triple_count], triple_grads, preferred_element_ty...]
    ppermute x0 -> x7, waiting for transfers between devices: none -> 7.8 us  [shards(): lax.ppermute(piece, 'owner', [(i, i ^ step) for i in range(owner_count)])]
    ppermute x1, waiting for transfers between devices: 7.75 us -> 11.9 us  [group_sums(): arrived.append(lax.ppermute(total.astype(jnp.bfloat16), 'blk', route))]
  transfers between devices with their start and end apart: 14 -> 21, of which waited for: 4 -> 8; matrix products, arithmetic and copies ran while one was open for 18% -> 23% of each run, Pallas kernels for 0% -> 0%
where the time goes in v2:
time: 337 us
  waiting for transfers between devices  159 us (47%)
  matrix products  74.9 us (22%)
  local copies, waits for them, and re-layouts  37 us (11%)
  starting transfers between devices  29.6 us (9%)
  other arithmetic  21.7 us (6%)
  blocking collectives  13.7 us (4%)
    all_to_all x1, waiting for transfers between devices, shards(): lax.all_to_all(outgoing, 'owner', split_axis=0, concat_axis=0, tiled=True)  76.7 us
    all_to_all x1, waiting for transfers between devices, shards(): lax.all_to_all(found_rows, 'owner', split_axis=0, concat_axis=0, tiled=True)  57.8 us
    dot_general x1, matrix products, shards(): jnp.dot(packing[:, :2 * triple_count], triple_grads, preferred_element_ty...  23.4 us
    gather x1, local copies, waits for them, and re-layouts, shards(): found_rows = entity_table.at[asked_rows].get(mode='promise_in_bounds')  18.6 us
    dot_general x4, matrix products, block(): return jnp.dot(landing, grads, preferred_element_type=jnp.float32)  16.6 us
    eq x1, other arithmetic, shards(): packing = (slots[:, None] == target[None, :]).astype(jnp.bfloat16)  14.4 us
    all_to_all x1, blocking collectives, shards(): lax.all_to_all(requests, 'owner', split_axis=0, concat_axis=0, tiled=True)  13.7 us
    ppermute x7, starting transfers between devices, shards(): lax.ppermute(piece, 'owner', [(i, i ^ step) for i in range(owner_count)])  13.6 us
  transfers between devices with their start and end apart: 21, of which 8 were waited for; matrix products, arithmetic and copies ran while one was open for 23% of the time, Pallas kernels for 0%

profile of v2, /device:TPU:0, one launch (start us, length us, event | category | flops | bytes accessed | tf_op | source)
XLA Modules:
  0.0 337.2 jit_solution(3796560993525587089)
XLA Ops:
  0.6 0.8 constant_dynamic-update-slice_fusion.2
  2.9 0.8 fusion.85
  4.3 11.4 %convolution_convert_fusion = s32[6400,2]{0,1:T(2,128)S(1)} fusion(s32[2560]{0:T(1024)S(1)} %fusion.69, bf16[2560,1]{0,1:T(2,128)(2,1)S(1)} %fusion.76, bf16[2560,1]{0,1:T(2,128)(2,1)S(1)} %get-tuple-element.4), kind=kOutput, calls=%fused_computation.26 | convolution fusion | flops 81953280 | bytes 71680 | tf_op jit(solution)/shard_map/dot_general | solution.py:69
  15.9 13.7 %all_to_all.22 = s32[8,1,800]{2,1,0:T(1,128)S(1)} all-to-all(s32[8,1,800]{2,1,0:T(1,128)S(1)} %add.346), channel_id=1, replica_groups=mesh['owner'=8,'blk'=4] {'owner'}, dimensions={0} | all-to-all | bytes 51200 | tf_op jit(solution)/shard_map/all_to_all | solution.py:71
  30.5 18.6 %gather_fusion = bf16[6400,256]{1,0:T(8,128)(2,1)} fusion(bf16[4096,256]{1,0:T(8,128)(2,1)S(1)} %copy-done, s32[7168]{0:T(1024)S(1)} %pad_clamp_fusion), kind=kCustom, calls=%fused_computation | custom fusion | bytes 6579200 | tf_op jit(solution)/shard_map/gather | solution.py:72
  49.1 3.8 %all-to-all-start.1 = ((bf16[8,800,256]{2,1,0:T(8,128)(2,1)}), bf16[8,800,256]{2,1,0:T(8,128)(2,1)S(1)}, u32[]{:S(2)}, u32[]{:S(2)}) async-start(bf16[8,800,256]{2,1,0:T(8,128)(2,1)} %bitcast.126), calls=%async_computation.1 | async-start | bytes 6553600 | tf_op jit(solution)/shard_map/all_to_all | solution.py:74
  53.0 14.4 %iota_compare_fusion = pred[6400,2560]{1,0:T(32,128)(4,1)} fusion(s32[2560]{0:T(1024)S(1)} %fusion.69), kind=kLoop, calls=%fused_computation.2 | loop fusion | flops 16384000 | bytes 16394240 | tf_op jit(solution)/shard_map/eq | solution.py:67
  67.4 57.8 %all-to-all-done.1 = bf16[8,800,256]{2,1,0:T(8,128)(2,1)S(1)} async-done(((bf16[8,800,256]{2,1,0:T(8,128)(2,1)}), bf16[8,800,256]{2,1,0:T(8,128)(2,1)S(1)}, u32[]{:S(2)}, u32[]{:S(2)}) %all-to-all-start.1) | async-done | bytes 3276832 | tf_op jit(solution)/shard_map/all_to_all | solution.py:74
  125.2 8.4 %gather_fusion.1 = bf16[2560,256]{1,0:T(8,128)(2,1)} fusion(bf16[6400,256]{1,0:T(8,128)(2,1)S(1)} %bitcast.125, s32[3072]{0:T(1024)S(1)} %pad_clamp_fusion.1), kind=kCustom, calls=%fused_computation.1 | custom fusion | bytes 2631680 | tf_op jit(solution)/shard_map/gather | solution.py:78
  133.6 1.7 slice.41
  135.2 1.6 collective-permute-start.2
  137.4 1.1 slice.39
  138.7 2.3 broadcast_multiply_fusion
  141.0 1.4 fusion.46
  142.4 0.8 multiply_convert_fusion.3
  144.6 1.2 convolution_convert_fusion.1
  145.8 1.8 collective-permute-start.5
  147.6 2.8 collective-permute-done.1
  150.3 1.7 multiply_convert_fusion.1
  152.0 1.2 convolution_convert_fusion.2
  153.2 1.6 collective-permute-start.4
  155.6 1.2 convolution_convert_fusion.3
  157.2 1.4 fusion.88
  159.0 1.0 copy.17
  160.0 3.6 %fusion.54 = f32[4,512,256]{2,1,0:T(8,128)S(1)} fusion(bf16[4,512,1024]{2,1,0:T(8,128)(2,1)} %bitcast.127, bf16[1024,256]{1,0:T(8,128)(2,1)S(1)} %fusion.38), kind=kOutput, calls=%fused_computation.67 | convolution fusion | flops 1073741824 | bytes 6815744 | tf_op jit(solution)/shard_map/dot_general | solution.py:120
  164.4 1.4 fusion.39
  165.8 1.6 collective-permute-start.7
  167.4 23.4 %fusion.23 = bf16[6400,256]{1,0:T(8,128)(2,1)} fusion(pred[6400,2560]{1,0:T(32,128)(4,1)} %iota_compare_fusion, bf16[1024,256]{1,0:T(8,128)(2,1)S(1)} %fusion.47, bf16[1024,256]{1,0:T(8,128)(2,1)S(1)} %fusion.39), kind=kOutput, calls=%fused_computation.24 | convolution fusion | flops 6714621952 | bytes 17432576 | tf_op jit(solution)/shard_map/dot_general | solution.py:135
  191.0 6.6 %fusion.26 = bf16[6400,256]{1,0:T(8,128)(2,1)S(1)} fusion(bf16[6400,256]{1,0:T(8,128)(2,1)} %fusion.23, pred[6400,2560]{1,0:T(32,128)(4,1)} %iota_compare_fusion, bf16[512,256]{1,0:T(8,128)(2,1)} %collective-permute-done.5, bf16[512,256]{1,0:T(8,128)(2,1)} %collective-permute-done.4, bf16[512,256]{1,0:T(8,128)(2,1)} %collective-permute-done.3, ...), kind=kOutput, calls=%fused_computation.25 | convolution fusion | flops 1955266560 | bytes 12189696 | tf_op jit(solution)/shard_map/dot_general | solution.py:140
  197.6 2.0 pad_maximum_fusion
  199.6 3.7 %all-to-all-start.2 = ((bf16[8,864,256]{2,1,0:T(8,128)(2,1)}), bf16[8,864,256]{2,1,0:T(8,128)(2,1)S(1)}, u32[]{:S(2)}, u32[]{:S(2)}) async-start(bf16[8,864,256]{2,1,0:T(8,128)(2,1)} %pad_maximum_fusion), calls=%async_computation.2 | async-start | bytes 7077888 | tf_op jit(solution)/shard_map/all_to_all | solution.py:147
  204.8 1.4 eq.107
  206.2 76.7 %all-to-all-done.2 = bf16[8,864,256]{2,1,0:T(8,128)(2,1)S(1)} async-done(((bf16[8,864,256]{2,1,0:T(8,128)(2,1)}), bf16[8,864,256]{2,1,0:T(8,128)(2,1)S(1)}, u32[]{:S(2)}, u32[]{:S(2)}) %all-to-all-start.2) | async-done | bytes 3538976 | tf_op jit(solution)/shard_map/all_to_all | solution.py:147
  283.0 2.4 collective-permute-start.18
  285.4 2.4 collective-permute-start.17
  288.3 4.7 %fusion.2 = f32[1024,256]{1,0:T(8,128)S(1)} fusion(bf16[6912,256]{1,0:T(8,128)(2,1)S(1)} %bitcast.128, s32[6912]{0:T(1024)} %eq.107, s32[1024]{0:T(1024)S(1)} %iota_add_fusion), kind=kOutput, calls=%fused_computation.5 | convolution fusion | flops 3630956544 | bytes 4619264 | tf_op jit(solution)/shard_map/dot_general | solution.py:34
  293.0 3.9 %fusion.4 = f32[1024,256]{1,0:T(8,128)S(1)} fusion(bf16[6912,256]{1,0:T(8,128)(2,1)S(1)} %bitcast.129, s32[6912]{0:T(1024)S(1)} %copy-done.7, s32[1024]{0:T(1024)S(1)} %iota_add_fusion.1), kind=kOutput, calls=%fused_computation.7 | convolution fusion | flops 3630956544 | bytes 4619264 | tf_op jit(solution)/shard_map/dot_general | solution.py:34
  296.9 4.1 %fusion.6 = f32[1024,256]{1,0:T(8,128)S(1)} fusion(bf16[6912,256]{1,0:T(8,128)(2,1)S(1)} %bitcast.130, s32[6912]{0:T(1024)S(1)} %copy-done.7, s32[1024]{0:T(1024)S(1)} %iota_add_fusion.2), kind=kOutput, calls=%fused_computation.9 | convolution fusion | flops 3630956544 | bytes 4619264 | tf_op jit(solution)/shard_map/dot_general | solution.py:34
  301.1 3.9 %fusion.8 = f32[1024,256]{1,0:T(8,128)S(1)} fusion(bf16[6912,256]{1,0:T(8,128)(2,1)S(1)} %bitcast.131, s32[6912]{0:T(1024)S(1)} %copy-done.7, s32[1024]{0:T(1024)S(1)} %iota_add_fusion.3), kind=kOutput, calls=%fused_computation.11 | convolution fusion | flops 3630956544 | bytes 4619264 | tf_op jit(solution)/shard_map/dot_general | solution.py:34
  305.1 3.0 collective-permute-start.13
  308.1 2.7 collective-permute-done.13
  310.9 2.6 collective-permute-start.14
  313.5 2.6 collective-permute-done.14
  316.0 2.7 collective-permute-start.15
  318.7 2.5 collective-permute-done.15
  322.1 1.8 collective-permute-done.9
  323.8 11.9 %collective-permute-done.11 = bf16[1024,256]{1,0:T(8,128)(2,1)S(1)} collective-permute-done((bf16[1024,256]{1,0:T(8,128)(2,1)S(1)}, bf16[1024,256]{1,0:T(8,128)(2,1)S(1)}, u32[]{:S(2)}, u32[]{:S(2)}) %collective-permute-start.11) | collective-permute-done | bytes 524320 | tf_op jit(solution)/shard_map/ppermute | solution.py:43
  335.8 1.1 convert_add_fusion
  (92 shorter events, 10.7 us)
Async XLA Ops:
  0.6 29.9 %copy-start = (bf16[4096,256]{1,0:T(8,128)(2,1)S(1)}, bf16[4096,256]{1,0:T(8,128)(2,1)}, u32[]{:S(2)}) copy-start(bf16[4096,256]{1,0:T(8,128)(2,1)} %param.6) | copy-start | bytes 6291460
  29.7 0.6 copy-start.6
  49.1 3.8 %copy-start.8 = (s32[1024]{0:T(1024)S(1)}, s32[1024]{0:T(1024)}, u32[]{:S(2)}) copy-start(s32[1024]{0:T(1024)} %param.9) | copy-start | bytes 12292
  49.1 76.1 %all-to-all-start.1 = ((bf16[8,800,256]{2,1,0:T(8,128)(2,1)}), bf16[8,800,256]{2,1,0:T(8,128)(2,1)S(1)}, u32[]{:S(2)}, u32[]{:S(2)}) async-start(bf16[8,800,256]{2,1,0:T(8,128)(2,1)} %bitcast.126), calls=%async_computation.1 | async-start | bytes 6553600 | tf_op jit(solution)/shard_map/all_to_all | solution.py:74
  135.2 5.7 %copy-start.2 = (bf16[2560,256]{1,0:T(8,128)(2,1)S(1)}, bf16[2560,256]{1,0:T(8,128)(2,1)}, u32[]{:S(2)}) copy-start(bf16[2560,256]{1,0:T(8,128)(2,1)} %gather_fusion.1) | copy-start | bytes 3932164
  135.2 19.6 %collective-permute-start = (bf16[512,256]{1,0:T(8,128)(2,1)}, bf16[512,256]{1,0:T(8,128)(2,1)S(1)}, u32[]{:S(2)}, u32[]{:S(2)}) collective-permute-start(bf16[512,256]{1,0:T(8,128)(2,1)} %slice.41), channel_id=1, source_target_pairs={{0,1},{1,0},{2,3},{3,2},{4,5},{5,4},{6,7},{7,6},{8,9},{9,8},{10,11... | collective-permute-start | bytes 786440 | tf_op jit(solution)/shard_map/ppermute | solution.py:85
  135.2 8.6 %collective-permute-start.2 = (bf16[512,256]{1,0:T(8,128)(2,1)}, bf16[512,256]{1,0:T(8,128)(2,1)S(1)}, u32[]{:S(2)}, u32[]{:S(2)}) collective-permute-start(bf16[512,256]{1,0:T(8,128)(2,1)} %slice.41), channel_id=1, source_target_pairs={{0,3},{1,2},{2,1},{3,0},{4,7},{5,6},{6,5},{7,4},{8,11},{9,10},{10,... | collective-permute-start | bytes 786440 | tf_op jit(solution)/shard_map/ppermute | solution.py:85
  136.8 13.5 %collective-permute-start.1 = (bf16[512,256]{1,0:T(8,128)(2,1)}, bf16[512,256]{1,0:T(8,128)(2,1)}, u32[]{:S(2)}, u32[]{:S(2)}) collective-permute-start(bf16[512,256]{1,0:T(8,128)(2,1)} %slice.41), channel_id=1, source_target_pairs={{0,2},{1,3},{2,0},{3,1},{4,6},{5,7},{6,4},{7,5},{8,10},{9,11},{10,... | collective-permute-start | bytes 786440 | tf_op jit(solution)/shard_map/ppermute | solution.py:85
  138.7 2.3 copy-start.9
  142.4 13.2 %copy-start.4 = (bf16[1024,256]{1,0:T(8,128)(2,1)}, bf16[1024,256]{1,0:T(8,128)(2,1)S(1)}, u32[]{:S(2)}) copy-start(bf16[1024,256]{1,0:T(8,128)(2,1)S(1)} %get-tuple-element.12) | copy-start | bytes 1572868
  143.2 1.4 copy-start.11
  145.8 45.1 %collective-permute-start.5 = (bf16[512,256]{1,0:T(8,128)(2,1)}, bf16[512,256]{1,0:T(8,128)(2,1)}, u32[]{:S(2)}, u32[]{:S(2)}) collective-permute-start(bf16[512,256]{1,0:T(8,128)(2,1)} %convolution_convert_fusion.1), channel_id=1, source_target_pairs={{0,3},{1,2},{2,1},{3,0},{4,7},{5,6},{6,5},{7,4},{8,11},{9,10},{10,... | collective-permute-start | bytes 786440 | tf_op jit(solution)/shard_map/ppermute | solution.py:113
  153.2 37.7 %collective-permute-start.4 = (bf16[512,256]{1,0:T(8,128)(2,1)}, bf16[512,256]{1,0:T(8,128)(2,1)}, u32[]{:S(2)}, u32[]{:S(2)}) collective-permute-start(bf16[512,256]{1,0:T(8,128)(2,1)} %convolution_convert_fusion.2), channel_id=1, source_target_pairs={{0,2},{1,3},{2,0},{3,1},{4,6},{5,7},{6,4},{7,5},{8,10},{9,11},{10,... | collective-permute-start | bytes 786440 | tf_op jit(solution)/shard_map/ppermute | solution.py:113
  156.7 34.2 %collective-permute-start.3 = (bf16[512,256]{1,0:T(8,128)(2,1)}, bf16[512,256]{1,0:T(8,128)(2,1)}, u32[]{:S(2)}, u32[]{:S(2)}) collective-permute-start(bf16[512,256]{1,0:T(8,128)(2,1)} %convolution_convert_fusion.3), channel_id=1, source_target_pairs={{0,1},{1,0},{2,3},{3,2},{4,5},{5,4},{6,7},{7,6},{8,9},{9,8},{10,11... | collective-permute-start | bytes 786440 | tf_op jit(solution)/shard_map/ppermute | solution.py:113
  160.0 4.4 %copy-start.5 = (bf16[1024,256]{0,1:T(8,128)(2,1)S(1)}, bf16[1024,256]{0,1:T(8,128)(2,1)}, u32[]{:S(2)}) copy-start(bf16[1024,256]{0,1:T(8,128)(2,1)} %copy.17) | copy-start | bytes 1572868
  160.0 4.4 %copy-start.10 = (bf16[8,256,256]{2,1,0:T(8,128)(2,1)S(1)}, bf16[8,256,256]{2,1,0:T(8,128)(2,1)}, u32[]{:S(2)}) copy-start(bf16[8,256,256]{2,1,0:T(8,128)(2,1)} %param.7) | copy-start | bytes 3145732
  163.7 2.1 collective-permute-start.6
  164.3 26.5 %collective-permute-start.8 = (bf16[512,256]{1,0:T(8,128)(2,1)S(1)}, bf16[512,256]{1,0:T(8,128)(2,1)S(1)}, u32[]{:S(2)}, u32[]{:S(2)}) collective-permute-start(bf16[512,256]{1,0:T(8,128)(2,1)S(1)} %get-tuple-element.9), channel_id=1, source_target_pairs={{0,3},{1,2},{2,1},{3,0},{4,7},{5,6},{6,5},{7,4},{8,11},{9,10},{10,... | collective-permute-start | bytes 786440 | tf_op jit(solution)/shard_map/ppermute | solution.py:131
  165.8 25.0 %collective-permute-start.7 = (bf16[512,256]{1,0:T(8,128)(2,1)S(1)}, bf16[512,256]{1,0:T(8,128)(2,1)S(1)}, u32[]{:S(2)}, u32[]{:S(2)}) collective-permute-start(bf16[512,256]{1,0:T(8,128)(2,1)S(1)} %get-tuple-element.10), channel_id=1, source_target_pairs={{0,2},{1,3},{2,0},{3,1},{4,6},{5,7},{6,4},{7,5},{8,10},{9,11},{10,... | collective-permute-start | bytes 786440 | tf_op jit(solution)/shard_map/ppermute | solution.py:131
  199.6 83.3 %all-to-all-start.2 = ((bf16[8,864,256]{2,1,0:T(8,128)(2,1)}), bf16[8,864,256]{2,1,0:T(8,128)(2,1)S(1)}, u32[]{:S(2)}, u32[]{:S(2)}) async-start(bf16[8,864,256]{2,1,0:T(8,128)(2,1)} %pad_maximum_fusion), calls=%async_computation.2 | async-start | bytes 7077888 | tf_op jit(solution)/shard_map/all_to_all | solution.py:147
  283.0 39.1 %collective-permute-start.18 = (f32[64,256]{1,0:T(8,128)S(1)}, f32[64,256]{1,0:T(8,128)S(1)}, u32[]{:S(2)}, u32[]{:S(2)}) collective-permute-start(f32[64,256]{1,0:T(8,128)S(1)} %convert_reduce_fusion), channel_id=1, source_target_pairs={{0,28},{4,24},{8,20},{12,16},{16,12},{20,8},{24,4},{28,0},{1,29},{... | collective-permute-start | bytes 196616 | tf_op jit(solution)/shard_map/ppermute | solution.py:154
  285.4 36.7 %collective-permute-start.17 = (f32[64,256]{1,0:T(8,128)S(1)}, f32[64,256]{1,0:T(8,128)S(1)}, u32[]{:S(2)}, u32[]{:S(2)}) collective-permute-start(f32[64,256]{1,0:T(8,128)S(1)} %convert_reduce_fusion), channel_id=1, source_target_pairs={{0,24},{4,28},{8,16},{12,20},{16,8},{20,12},{24,0},{28,4},{1,25},{... | collective-permute-start | bytes 196616 | tf_op jit(solution)/shard_map/ppermute | solution.py:154
  287.8 34.2 %collective-permute-start.16 = (f32[64,256]{1,0:T(8,128)S(1)}, f32[64,256]{1,0:T(8,128)S(1)}, u32[]{:S(2)}, u32[]{:S(2)}) collective-permute-start(f32[64,256]{1,0:T(8,128)S(1)} %convert_reduce_fusion), channel_id=1, source_target_pairs={{0,20},{4,16},{8,28},{12,24},{16,4},{20,0},{24,12},{28,8},{1,21},{... | collective-permute-start | bytes 196616 | tf_op jit(solution)/shard_map/ppermute | solution.py:154
  287.8 17.4 %collective-permute-start.12 = (f32[64,256]{1,0:T(8,128)S(1)}, f32[64,256]{1,0:T(8,128)S(1)}, u32[]{:S(2)}, u32[]{:S(2)}) collective-permute-start(f32[64,256]{1,0:T(8,128)S(1)} %convert_reduce_fusion), channel_id=1, source_target_pairs={{0,4},{4,0},{8,12},{12,8},{16,20},{20,16},{24,28},{28,24},{1,5},{5... | collective-permute-start | bytes 196616 | tf_op jit(solution)/shard_map/ppermute | solution.py:154
  288.3 4.7 %copy-start.7 = (s32[6912]{0:T(1024)S(1)}, s32[6912]{0:T(1024)}, u32[]{:S(2)}) copy-start(s32[6912]{0:T(1024)} %eq.107) | copy-start | bytes 82948
  305.0 16.2 %collective-permute-start.10 = (f32[1024,256]{1,0:T(8,128)S(1)}, f32[1024,256]{1,0:T(8,128)S(1)}, u32[]{:S(2)}, u32[]{:S(2)}) collective-permute-start(f32[1024,256]{1,0:T(8,128)S(1)} %fusion.2), channel_id=1, source_target_pairs={{0,1},{1,0},{2,3},{3,2},{4,5},{5,4},{6,7},{7,6},{8,9},{9,8},{10,11... | collective-permute-start | bytes 3145736 | tf_op jit(solution)/shard_map/ppermute | solution.py:39
  305.1 5.7 %collective-permute-start.13 = (f32[64,256]{1,0:T(8,128)S(1)}, f32[64,256]{1,0:T(8,128)S(1)}, u32[]{:S(2)}, u32[]{:S(2)}) collective-permute-start(f32[64,256]{1,0:T(8,128)S(1)} %convert_reduce_fusion), channel_id=1, source_target_pairs={{0,8},{4,12},{8,0},{12,4},{16,24},{20,28},{24,16},{28,20},{1,9},{5... | collective-permute-start | bytes 196616 | tf_op jit(solution)/shard_map/ppermute | solution.py:154
  308.1 28.8 %copy-start.1 = (bf16[4096,256]{1,0:T(8,128)(2,1)S(1)}, bf16[4096,256]{1,0:T(8,128)(2,1)}, u32[]{:S(2)}) copy-start(bf16[4096,256]{1,0:T(8,128)(2,1)} %param.6) | copy-start | bytes 6291460
  310.9 5.2 %collective-permute-start.14 = (f32[64,256]{1,0:T(8,128)S(1)}, f32[64,256]{1,0:T(8,128)S(1)}, u32[]{:S(2)}, u32[]{:S(2)}) collective-permute-start(f32[64,256]{1,0:T(8,128)S(1)} %convert_reduce_fusion), channel_id=1, source_target_pairs={{0,12},{4,8},{8,4},{12,0},{16,28},{20,24},{24,20},{28,16},{1,13},{... | collective-permute-start | bytes 196616 | tf_op jit(solution)/shard_map/ppermute | solution.py:154
  316.0 5.2 %collective-permute-start.15 = (f32[64,256]{1,0:T(8,128)S(1)}, f32[64,256]{1,0:T(8,128)S(1)}, u32[]{:S(2)}, u32[]{:S(2)}) collective-permute-start(f32[64,256]{1,0:T(8,128)S(1)} %convert_reduce_fusion), channel_id=1, source_target_pairs={{0,16},{4,20},{8,24},{12,28},{16,0},{20,4},{24,8},{28,12},{1,17},{... | collective-permute-start | bytes 196616 | tf_op jit(solution)/shard_map/ppermute | solution.py:154
  321.2 2.7 collective-permute-start.9
  321.4 14.4 %collective-permute-start.11 = (bf16[1024,256]{1,0:T(8,128)(2,1)S(1)}, bf16[1024,256]{1,0:T(8,128)(2,1)S(1)}, u32[]{:S(2)}, u32[]{:S(2)}) collective-permute-start(bf16[1024,256]{1,0:T(8,128)(2,1)S(1)} %add_convert_fusion), channel_id=1, source_target_pairs={{0,2},{1,3},{2,0},{3,1},{4,6},{5,7},{6,4},{7,5},{8,10},{9,11},{10,... | collective-permute-start | bytes 1572872 | tf_op jit(solution)/shard_map/ppermute | solution.py:43
  322.1 14.8 %copy-start.3 = (f32[8,64,256]{2,1,0:T(8,128)}, f32[8,64,256]{2,1,0:T(8,128)S(1)}, u32[]{:S(2)}) copy-start(f32[8,64,256]{2,1,0:T(8,128)S(1)} %bitcast_dynamic-update-slice_fusion) | copy-start | bytes 1572868
